TPU v7x, 512 devices: a whole 4x8x8 slice. The times are simulated.
512 devices in a mesh: dp: 2 (over z_hi), row: 8 (over z_lo, core), col: 32 (over x, y).
Axes of the slice: x: 4, y: 8, z: 8 (z_hi: 2, z_lo: 4; z = z_hi * 4 + z_lo), core: 2. Of those that a mesh axis runs over, the one named last changes fastest.
Arguments:
- grads: bfloat16 [2, 4, 6144, 6144], P('dp', None, 'col', 'row'), as said below
- params: float32 [4, 6144, 6144], P('dp', 'col', 'row'), may hold values from -6 to 6
- row_moments: float32 [4, 6144], P('dp', 'row'), may hold values from 0.2 to 5
- col_moments: float32 [4, 6144], P('dp', 'col'), may hold values from 0.2 to 5
Outputs:
- new_params: float32 [4, 6144, 6144], P('dp', 'col', 'row')
- update: float32 [4, 6144, 6144], P('dp', 'col', 'row')
- new_row_moments: float32 [4, 6144], P('dp', 'row')
- new_col_moments: float32 [4, 6144], P('dp', 'col')
- row_mean: float32 [4], P('dp')
Inputs may be any that keep to these rules, and one draw needn't show every extreme that they name: `grads`: each replica's share of the gradient, finite.
All inputs are finite; a program needn't handle non-finite values.
Results may differ from a plain program's by a relative error of at most 0.0003.
Values sent between devices are 32-bit elements; how exact they have to be, the bound alone decides.
No kernel may reach another device: no remote copies, remote signals or barrier semaphores. Data moves between devices by JAX's collectives and lax.ppermute only.
A program may use at most 64 MiB of HBM per device.

v0:
```python
import jax
import jax.numpy as jnp
from jax import lax
from jax.sharding import PartitionSpec as P

D = 6144


def local_pass(grad):
    square = grad * grad + 1e-30
    row_part = jnp.sum(square, axis=1)
    col_part = jnp.sum(square, axis=2)
    return (row_part, col_part, jnp.sum(row_part, axis=1))


def per_device(grads, params, row_moments, col_moments):
    shares = grads[0]
    grad = lax.psum_scatter(shares.astype(jnp.float32), "dp", scatter_dimension=0, tiled=True)
    row_part, col_part, total_part = local_pass(grad)
    width = jnp.float32(D)
    row_sum = lax.psum(row_part, "col")
    col_sum = lax.psum(col_part, "row")
    new_rows = 0.8 * row_moments + 0.2 * (row_sum / width)
    new_cols = 0.8 * col_moments + 0.2 * (col_sum / width)
    row_mean = lax.psum(jnp.sum(new_rows, axis=1), "row") / width
    raw = grad * lax.rsqrt(new_cols[:, :, None] * new_rows[:, None, :] / row_mean[:, None, None])
    squares_sum = lax.psum(jnp.sum(raw * raw, axis=(1, 2)), ("row", "col"))
    clip = jnp.maximum(jnp.float32(1.0), jnp.sqrt(squares_sum / (width * width)))
    update = raw / clip[:, None, None]
    return (params - 0.01 * update, update, new_rows, new_cols, row_mean)


def solution(mesh):
    return jax.shard_map(
        per_device,
        mesh=mesh,
        in_specs=(
            P("dp", None, "col", "row"),
            P("dp", "col", "row"),
            P("dp", "row"),
            P("dp", "col"),
        ),
        out_specs=(
            P("dp", "col", "row"),
            P("dp", "col", "row"),
            P("dp", "row"),
            P("dp", "col"),
            P("dp"),
        ),
        check_vma=False,
    )
```

profile of v0, /device:TPU:8, one launch (start us, length us, event | category | flops | bytes accessed | tf_op | source)
XLA Modules:
  0.0 854.1 jit_solution(14449069298675209560)
XLA Ops:
  7.2 0.0 reduce-scatter.2.cloned.1.call-start
  7.2 2.9 bitcast_convert_fusion
  10.1 0.0 reduce-scatter.2.cloned.1.call-update
  10.1 0.0 copy-start.4
  10.1 0.0 copy-start.5
  10.1 78.0 %reduce-scatter.2.cloned.1.call-done = f32[2,192,768]{2,1,0:T(8,128)} async-done(((f32[4,192,768]{2,1,0:T(8,128)}), f32[2,192,768]{2,1,0:T(8,128)}) %reduce-scatter.2.cloned.1.call-update) | async-done | bytes 1179664 | tf_op jit(solution)/shard_map/reduce_scatter | solution.py:18
  88.1 0.0 copy-start
  88.1 0.0 copy-start.1
  88.1 1.7 fusion.1
  89.8 72.3 %psum.29 = f32[2,768]{1,0:T(2,128)S(1)} all-reduce(f32[2,768]{1,0:T(2,128)S(1)} %get-tuple-element.6), channel_id=1, replica_groups=mesh['dp'=2,'row'=8,'col'=32] {'col'}, use_global_device_ids=true, to_apply=%region_4.0 | all-reduce | flops 1536 | bytes 12288 | tf_op jit(solution)/shard_map/psum | solution.py:21
  162.1 0.0 copy-done.4
  162.1 0.1 fusion.2
  162.2 0.0 copy-start.2
  162.2 13.6 %all-reduce = (f32[2]{0:T(128)S(1)}, f32[2,192]{1,0:T(2,128)S(1)}) all-reduce(f32[2]{0:T(128)S(1)} %get-tuple-element.11, f32[2,192]{1,0:T(2,128)S(1)} %get-tuple-element.5), channel_id=1, replica_groups=mesh['dp'=2,'row'=8,'col'=32] {'row'}, use_global_device_ids=true, to_apply=%region_6.0 | all-reduce | flops 386 | bytes 3088 | tf_op jit(solution)/shard_map/psum | solution.py:25
  175.8 0.0 copy-start.6
  175.8 0.0 copy-done.5
  175.9 0.0 copy-start.3
  175.9 0.0 copy-done
  175.9 0.5 multiply_reduce_fusion
  176.4 669.1 %psum.31 = f32[2]{0:T(128)S(1)} all-reduce(f32[2]{0:T(128)S(1)} %multiply_reduce_fusion), channel_id=1, replica_groups=mesh['dp'=2,'row'=8,'col'=32] {'row','col'}, use_global_device_ids=true, to_apply=%region_8.0 | all-reduce | flops 2 | bytes 16 | tf_op jit(solution)/shard_map/psum | solution.py:27
  845.5 0.0 copy-done.1
  845.5 1.8 multiply_subtract_fusion
  847.2 0.0 copy-done.2
  847.2 0.0 copy-done.6
  847.2 0.0 copy-done.3
  (3 shorter events, 0.0 us)
Async XLA Ops:
  7.2 80.9 %reduce-scatter.2.cloned.1.call-start = ((), (), s32[]{:S(2)}) async-start(), calls=%async_computation.1 | async-start | bytes 3538944 | tf_op jit(solution)/shard_map/reduce_scatter | solution.py:18
  10.1 152.0 %copy-start.4 = (f32[2,768]{1,0:T(2,128)S(1)}, f32[2,768]{1,0:T(2,128)}, u32[]{:S(2)}) copy-start(f32[2,768]{1,0:T(2,128)} %param.6) | copy-start | bytes 18436
  10.1 165.7 %copy-start.5 = (f32[2,192]{1,0:T(2,128)S(1)}, f32[2,192]{1,0:T(2,128)}, u32[]{:S(2)}) copy-start(f32[2,192]{1,0:T(2,128)} %param.7) | copy-start | bytes 4612
  88.1 87.8 %copy-start = (f32[2,192,768]{2,1,0:T(8,128)S(1)}, f32[2,192,768]{2,1,0:T(8,128)}, u32[]{:S(2)}) copy-start(f32[2,192,768]{2,1,0:T(8,128)} %reduce-scatter.2.cloned.1.call-done) | copy-start | bytes 3538948
  88.1 757.4 %copy-start.1 = (f32[2,192,768]{2,1,0:T(8,128)S(1)}, f32[2,192,768]{2,1,0:T(8,128)}, u32[]{:S(2)}) copy-start(f32[2,192,768]{2,1,0:T(8,128)} %param.5) | copy-start | bytes 3538948
  162.2 685.0 %copy-start.2 = (f32[2,768]{1,0:T(2,128)}, f32[2,768]{1,0:T(2,128)S(1)}, u32[]{:S(2)}) copy-start(f32[2,768]{1,0:T(2,128)S(1)} %get-tuple-element.12) | copy-start | bytes 18436
  175.8 671.4 %copy-start.6 = (f32[2]{0:T(128)}, f32[2]{0:T(128)S(1)}, u32[]{:S(2)}) copy-start(f32[2]{0:T(128)S(1)} %broadcast_multiply_fusion) | copy-start | bytes 28
  175.9 671.4 %copy-start.3 = (f32[2,192]{1,0:T(2,128)}, f32[2,192]{1,0:T(2,128)S(1)}, u32[]{:S(2)}) copy-start(f32[2,192]{1,0:T(2,128)S(1)} %multiply_add_fusion.2) | copy-start | bytes 4612
Sparse Core Ops, SparseCore 0:
  10.8 77.2 reduce-scatter.1
where the time goes:
time: 854 us
  blocking collectives  755 us (88%)
  waiting for transfers between devices  78 us (9%)
  between operations  14.1 us (2%)
    psum x1, blocking collectives, per_device(): squares_sum = lax.psum(jnp.sum(raw * raw, axis=(1, 2)), ('row', 'col'))  669 us
    reduce_scatter x1, waiting for transfers between devices, per_device(): lax.psum_scatter(shares.astype(jnp.float32), 'dp', scatter_dimension=0, t...  78 us
    psum x1, blocking collectives, per_device(): row_sum = lax.psum(row_part, 'col')  72.3 us
  transfers between devices with their start and end apart: 1, of which 1 were waited for; matrix products, arithmetic and copies ran while one was open for 0% of the time, Pallas kernels for 0%

commit v1 on v0

v1 whole, which is shorter than its diff:
```python
import jax
import jax.numpy as jnp
from jax import lax
from jax.sharding import PartitionSpec as P

D = 6144


def gather_sum(x, axis, size):
    copies = jnp.broadcast_to(x[None], (size,) + x.shape)
    return jnp.sum(lax.all_to_all(copies, axis, 0, 0, tiled=True), axis=0)


def per_device(n_row, n_col, grads, params, row_moments, col_moments):
    shares = grads[0]
    half = shares.shape[0] // 2
    me = lax.axis_index("dp")
    give = lax.dynamic_slice_in_dim(shares, (1 - me) * half, half, 0).astype(jnp.float32)
    got = lax.ppermute(give, "dp", [(0, 1), (1, 0)])
    keep = lax.dynamic_slice_in_dim(shares, me * half, half, 0).astype(jnp.float32)
    grad = keep + got

    width = jnp.float32(D)
    square = grad * grad + 1e-30
    row_part = jnp.sum(square, axis=1)
    col_part = jnp.sum(square, axis=2)
    new_cols = 0.8 * col_moments + 0.2 * (gather_sum(col_part, "row", n_row) / width)
    weighed = jnp.sum(grad * grad * (1.0 / new_cols)[:, :, None], axis=1)
    both = gather_sum(jnp.concatenate([row_part, weighed], axis=0), "col", n_col)
    new_rows = 0.8 * row_moments + 0.2 * (both[:half] / width)
    tail = jnp.concatenate([jnp.sum(new_rows, axis=1), jnp.sum(both[half:] / new_rows, axis=1)])
    total = gather_sum(tail, "row", n_row)
    row_mean = total[:half] / width
    squares_sum = row_mean * total[half:]
    clip = jnp.maximum(jnp.float32(1.0), jnp.sqrt(squares_sum / (width * width)))
    scale = lax.rsqrt(new_cols) * (jnp.sqrt(row_mean) / clip)[:, None]
    update = grad * lax.rsqrt(new_rows)[:, None, :] * scale[:, :, None]
    return (params - 0.01 * update, update, new_rows, new_cols, row_mean)


def solution(mesh):
    n_row, n_col = mesh.shape["row"], mesh.shape["col"]
    return jax.shard_map(
        lambda *args: per_device(n_row, n_col, *args),
        mesh=mesh,
        in_specs=(
            P("dp", None, "col", "row"),
            P("dp", "col", "row"),
            P("dp", "row"),
            P("dp", "col"),
        ),
        out_specs=(
            P("dp", "col", "row"),
            P("dp", "col", "row"),
            P("dp", "row"),
            P("dp", "col"),
            P("dp"),
        ),
        check_vma=False,
    )
```

time: 854 us -> 111 us (0.13)
  the two profiles are of different devices: /device:TPU:8 before, /device:TPU:1 now
where the time goes in v1:
time: 111 us
  blocking collectives  68 us (61%)
  waiting for transfers between devices  24.9 us (22%)
  starting transfers between devices  11.5 us (10%)
  other arithmetic  5.78 us (5%)
    all_to_all x3, blocking collectives, gather_sum(): return jnp.sum(lax.all_to_all(copies, axis, 0, 0, tiled=True), axis=0)  68 us
    ppermute x1, waiting for transfers between devices, per_device(): got = lax.ppermute(give, 'dp', [(0, 1), (1, 0)])  24.9 us
    ppermute x1, starting transfers between devices, per_device(): got = lax.ppermute(give, 'dp', [(0, 1), (1, 0)])  11.5 us
    sub x1, other arithmetic, per_device(): return (params - 0.01 * update, update, new_rows, new_cols, row_mean)  2.95 us
  transfers between devices with their start and end apart: 1, of which 1 were waited for; matrix products, arithmetic and copies ran while one was open for 0% of the time, Pallas kernels for 0%

profile of v1, /device:TPU:1, one launch (start us, length us, event | category | flops | bytes accessed | tf_op | source)
XLA Modules:
  0.0 110.9 jit_solution(15042265593128282928)
XLA Ops:
  0.6 0.0 copy-start
  0.6 1.2 %bitcast_convert_fusion = f32[2,192,768]{2,1,0:T(8,128)S(1)} fusion(bf16[1,4,192,768]{3,2,1,0:T(8,128)(2,1)} %param.4, s32[]{:T(128)S(6)} %select_n.7), kind=kLoop, calls=%fused_computation.6 | loop fusion | flops 294912 | bytes 1769476 | tf_op jit(solution)/shard_map/convert_element_type | solution.py:18
  1.9 0.0 copy-start.4
  1.9 11.5 %collective-permute-start = (f32[2,192,768]{2,1,0:T(8,128)S(1)}, f32[2,192,768]{2,1,0:T(8,128)S(1)}, u32[]{:S(2)}, u32[]{:S(2)}) collective-permute-start(f32[2,192,768]{2,1,0:T(8,128)S(1)} %bitcast_convert_fusion), channel_id=1, source_target_pairs={{0,256},{256,0},{1,257},{257,1},{2,258},{258,2},{3,259},{259,3},{4... | collective-permute-start | bytes 3538952 | tf_op jit(solution)/shard_map/ppermute | solution.py:19
  13.4 24.9 %collective-permute-done = f32[2,192,768]{2,1,0:T(8,128)S(1)} collective-permute-done((f32[2,192,768]{2,1,0:T(8,128)S(1)}, f32[2,192,768]{2,1,0:T(8,128)S(1)}, u32[]{:S(2)}, u32[]{:S(2)}) %collective-permute-start) | collective-permute-done | bytes 1179680 | tf_op jit(solution)/shard_map/ppermute | solution.py:19
  38.3 0.0 copy-done
  38.3 0.4 add_reduce_fusion.1
  38.7 35.8 %all_to_all.16 = f32[8,2,192]{2,1,0:T(2,128)S(1)} all-to-all(f32[8,2,192]{2,1,0:T(2,128)S(1)} %broadcast_in_dim.6), channel_id=1, replica_groups=mesh['dp'=2,'row'=8,'col'=32] {'row'}, dimensions={0} | all-to-all | bytes 24576 | tf_op jit(solution)/shard_map/all_to_all | solution.py:11
  74.5 0.0 copy-done.4
  74.5 0.0 copy-start.2
  74.5 0.2 multiply_reduce_fusion
  74.7 0.0 copy-start.3
  74.7 0.1 broadcast_in_dim.7
  74.8 20.9 %all_to_all.17 = f32[32,4,768]{2,1,0:T(4,128)S(1)} all-to-all(f32[32,4,768]{2,1,0:T(4,128)S(1)} %broadcast_in_dim.7), channel_id=1, replica_groups=mesh['dp'=2,'row'=8,'col'=32] {'col'}, dimensions={0} | all-to-all | bytes 786432 | tf_op jit(solution)/shard_map/all_to_all | solution.py:11
  95.7 0.1 reduce_sum.76
  95.8 0.0 copy-done.3
  95.8 0.0 copy-start.1
  95.8 0.1 fusion.2
  96.0 0.1 pad_maximum_fusion.1
  96.0 11.3 %all_to_all.18 = f32[8,1,4]{2,1,0:T(1,128)S(1)} all-to-all(f32[8,1,4]{2,1,0:T(1,128)S(1)} %broadcast_in_dim.8), channel_id=1, replica_groups=mesh['dp'=2,'row'=8,'col'=32] {'row'}, dimensions={0} | all-to-all | bytes 256 | tf_op jit(solution)/shard_map/all_to_all | solution.py:11
  107.4 0.5 maximum_divide_fusion
  107.9 0.0 copy-done.2
  107.9 0.1 rsqrt_multiply_fusion
  108.0 2.9 %multiply_subtract_fusion = (f32[2,192,768]{2,1,0:T(8,128)}, f32[2,192,768]{2,1,0:T(8,128)}) fusion(f32[2,192,768]{2,1,0:T(8,128)} %param.5, f32[2,192]{1,0:T(2,128)S(1)} %rsqrt_multiply_fusion, f32[2,768]{1,0:T(2,128)S(1)} %get-tuple-element.11, f32[2,192,768]{2,1,0:T(8,128)S(1)} %collective-permute-done, bf16[1,4,192,768]{3,2,1,0:T(8,128)(2,1)S(1)} %copy-done, ...), kind=kLoop, calls=%fused_computation.1 | loop fusion | flops 1769472 | bytes 5316100 | tf_op jit(solution)/shard_map/sub | solution.py:38
  110.9 0.0 copy-done.1
  (7 shorter events, 0.1 us)
Async XLA Ops:
  0.6 37.6 %copy-start = (bf16[1,4,192,768]{3,2,1,0:T(8,128)(2,1)S(1)}, bf16[1,4,192,768]{3,2,1,0:T(8,128)(2,1)}, u32[]{:S(2)}) copy-start(bf16[1,4,192,768]{3,2,1,0:T(8,128)(2,1)} %param.4) | copy-start | bytes 3538948
  1.9 72.6 %copy-start.4 = (f32[2,192]{1,0:T(2,128)S(1)}, f32[2,192]{1,0:T(2,128)}, u32[]{:S(2)}) copy-start(f32[2,192]{1,0:T(2,128)} %param.7) | copy-start | bytes 4612
  1.9 36.4 %collective-permute-start = (f32[2,192,768]{2,1,0:T(8,128)S(1)}, f32[2,192,768]{2,1,0:T(8,128)S(1)}, u32[]{:S(2)}, u32[]{:S(2)}) collective-permute-start(f32[2,192,768]{2,1,0:T(8,128)S(1)} %bitcast_convert_fusion), channel_id=1, source_target_pairs={{0,256},{256,0},{1,257},{257,1},{2,258},{258,2},{3,259},{259,3},{4... | collective-permute-start | bytes 3538952 | tf_op jit(solution)/shard_map/ppermute | solution.py:19
  74.5 33.5 %copy-start.2 = (f32[2,192]{1,0:T(2,128)}, f32[2,192]{1,0:T(2,128)S(1)}, u32[]{:S(2)}) copy-start(f32[2,192]{1,0:T(2,128)S(1)} %get-tuple-element.16) | copy-start | bytes 4612
  74.7 21.1 %copy-start.3 = (f32[2,768]{1,0:T(2,128)S(1)}, f32[2,768]{1,0:T(2,128)}, u32[]{:S(2)}) copy-start(f32[2,768]{1,0:T(2,128)} %param.6) | copy-start | bytes 18436
  95.8 15.1 %copy-start.1 = (f32[2,768]{1,0:T(2,128)}, f32[2,768]{1,0:T(2,128)S(1)}, u32[]{:S(2)}) copy-start(f32[2,768]{1,0:T(2,128)S(1)} %get-tuple-element.12) | copy-start | bytes 18436

commit v2 on v1

v2 whole, which is shorter than its diff:
```python
import jax
import jax.numpy as jnp
from jax import lax
from jax.sharding import PartitionSpec as P

D = 6144


def gather_sum(x, axis, size):
    copies = jnp.broadcast_to(x[None], (size,) + x.shape)
    return jnp.sum(lax.all_to_all(copies, axis, 0, 0, tiled=True), axis=0)


def per_device(n_row, n_col, grads, params, row_moments, col_moments):
    shares = grads[0]
    half = shares.shape[0] // 2
    me = lax.axis_index("dp")
    width = jnp.float32(D)

    def layer(first, k):
        return lax.dynamic_index_in_dim(shares, first * half + k, 0, keepdims=False).astype(jnp.float32)

    got, after = [], shares
    for k in range(half):
        got.append(lax.ppermute(layer(1 - me, k), "dp", [(0, 1), (1, 0)]))

    grad, new_rows, new_cols, tails = [], [], [], []
    for k in range(half):
        if k:
            got[k], new_rows[k - 1], tails[k - 1] = lax.optimization_barrier((got[k], new_rows[k - 1], tails[k - 1]))
        g = layer(me, k) + got[k]
        square = g * g + 1e-30
        row_part = jnp.sum(square, axis=0)
        col_part = jnp.sum(square, axis=1)
        cols = 0.8 * col_moments[k] + 0.2 * (gather_sum(col_part, "row", n_row) / width)
        weighed = jnp.sum(g * g * (1.0 / cols)[:, None], axis=0)
        both = gather_sum(jnp.stack([row_part, weighed]), "col", n_col)
        rows = 0.8 * row_moments[k] + 0.2 * (both[0] / width)
        grad.append(g)
        new_rows.append(rows)
        new_cols.append(cols)
        tails.append(jnp.stack([jnp.sum(rows), jnp.sum(both[1] / rows)]))

    total = gather_sum(jnp.stack(tails), "row", n_row)
    row_mean = total[:, 0] / width
    squares_sum = row_mean * total[:, 1]
    clip = jnp.maximum(jnp.float32(1.0), jnp.sqrt(squares_sum / (width * width)))
    scale = jnp.sqrt(row_mean) / clip
    update = jnp.stack(
        [
            grad[k] * lax.rsqrt(new_rows[k])[None, :] * (lax.rsqrt(new_cols[k]) * scale[k])[:, None]
            for k in range(half)
        ]
    )
    return (params - 0.01 * update, update, jnp.stack(new_rows), jnp.stack(new_cols), row_mean)


def solution(mesh):
    n_row, n_col = mesh.shape["row"], mesh.shape["col"]
    return jax.shard_map(
        lambda *args: per_device(n_row, n_col, *args),
        mesh=mesh,
        in_specs=(
            P("dp", None, "col", "row"),
            P("dp", "col", "row"),
            P("dp", "row"),
            P("dp", "col"),
        ),
        out_specs=(
            P("dp", "col", "row"),
            P("dp", "col", "row"),
            P("dp", "row"),
            P("dp", "col"),
            P("dp"),
        ),
        check_vma=False,
    )
```

time: 111 us -> 141 us (1.27)
  blocking collectives: 68 us -> 0 us
  starting transfers between devices: 11.5 us -> 72.1 us
  waiting for transfers between devices: 24.9 us -> 51.3 us
  other arithmetic: 5.78 us -> 11.2 us
  local copies, waits for them, and re-layouts: 0.1 us -> 4.98 us
    all_to_all x3 -> x0, blocking collectives: 68 us -> none  [gather_sum(): return jnp.sum(lax.all_to_all(copies, axis, 0, 0, tiled=True), axis=0)]
    all_to_all x0 -> x5, starting transfers between devices: none -> 53.6 us  [gather_sum(): return jnp.sum(lax.all_to_all(copies, axis, 0, 0, tiled=True), axis=0)]
    all_to_all x0 -> x5, waiting for transfers between devices: none -> 25.3 us  [gather_sum(): return jnp.sum(lax.all_to_all(copies, axis, 0, 0, tiled=True), axis=0)]
    ppermute x1 -> x2, starting transfers between devices: 11.5 us -> 18.5 us  [per_device(): got.append(lax.ppermute(layer(1 - me, k), 'dp', [(0, 1), (1, 0)]))]
    another operation x0 -> x8, other arithmetic: none -> 4.14 us  [the longest x2 1.38 us: per_device(): total = gather_sum(jnp.stack(tails), 'row', n_row)]
    broadcast_in_dim x3 -> x5, local copies, waits for them, and re-layouts: 0.07 us -> 3.29 us  [gather_sum(): copies = jnp.broadcast_to(x[None], (size,) + x.shape)]
    ppermute x1 -> x2, waiting for transfers between devices: 24.9 us -> 26 us  [per_device(): got.append(lax.ppermute(layer(1 - me, k), 'dp', [(0, 1), (1, 0)]))]
  transfers between devices with their start and end apart: 1 -> 7, of which waited for: 1 -> 7; matrix products, arithmetic and copies ran while one was open for 0% -> 3% of each run, Pallas kernels for 0% -> 0%
where the time goes in v2:
time: 141 us; the launch traced here: 140 us
  starting transfers between devices  72.1 us (51%)
  waiting for transfers between devices  51.3 us (36%)
  other arithmetic  11.2 us (8%)
  local copies, waits for them, and re-layouts  4.98 us (4%)
    all_to_all x5, starting transfers between devices, gather_sum(): return jnp.sum(lax.all_to_all(copies, axis, 0, 0, tiled=True), axis=0)  53.6 us
    ppermute x2, waiting for transfers between devices, per_device(): got.append(lax.ppermute(layer(1 - me, k), 'dp', [(0, 1), (1, 0)]))  26 us
    all_to_all x5, waiting for transfers between devices, gather_sum(): return jnp.sum(lax.all_to_all(copies, axis, 0, 0, tiled=True), axis=0)  25.3 us
    ppermute x2, starting transfers between devices, per_device(): got.append(lax.ppermute(layer(1 - me, k), 'dp', [(0, 1), (1, 0)]))  18.5 us
    broadcast_in_dim x5, local copies, waits for them, and re-layouts, gather_sum(): copies = jnp.broadcast_to(x[None], (size,) + x.shape)  3.29 us
  transfers between devices with their start and end apart: 7, of which 7 were waited for; matrix products, arithmetic and copies ran while one was open for 3% of the time, Pallas kernels for 0%

profile of v2, /device:TPU:1, one launch (start us, length us, event | category | flops | bytes accessed | tf_op | source)
XLA Modules:
  0.0 140.5 jit_solution(14166049774316874859)
XLA Ops:
  0.6 0.0 copy-start
  0.6 0.0 copy-start.3
  0.7 1.2 bitcast_convert_fusion.1
  1.9 11.5 %collective-permute-start = (f32[192,768]{1,0:T(8,128)S(1)}, f32[192,768]{1,0:T(8,128)S(1)}, u32[]{:S(2)}, u32[]{:S(2)}) collective-permute-start(f32[192,768]{1,0:T(8,128)S(1)} %get-tuple-element.27), channel_id=1, source_target_pairs={{0,256},{256,0},{1,257},{257,1},{2,258},{258,2},{3,259},{259,3},{4... | collective-permute-start | bytes 1769480 | tf_op jit(solution)/shard_map/ppermute | solution.py:25
  13.4 0.0 copy-start.2
  13.4 12.2 %collective-permute-done = f32[192,768]{1,0:T(8,128)S(1)} collective-permute-done((f32[192,768]{1,0:T(8,128)S(1)}, f32[192,768]{1,0:T(8,128)S(1)}, u32[]{:S(2)}, u32[]{:S(2)}) %collective-permute-start) | collective-permute-done | bytes 589856 | tf_op jit(solution)/shard_map/ppermute | solution.py:25
  25.6 0.0 copy-done
  25.6 0.2 add_reduce_fusion.3
  25.8 0.6 broadcast_in_dim.10
  26.4 18.4 %all-to-all-start = ((f32[8,1,192]{2,1,0:T(1,128)}), f32[8,1,192]{2,1,0:T(1,128)S(1)}, u32[]{:S(2)}, u32[]{:S(2)}) async-start(f32[8,1,192]{2,1,0:T(1,128)} %broadcast_in_dim.10), calls=%async_computation | async-start | bytes 16384 | tf_op jit(solution)/shard_map/all_to_all | solution.py:11
  44.8 0.0 copy-done.3
  44.9 4.9 %all-to-all-done = f32[8,1,192]{2,1,0:T(1,128)S(1)} async-done(((f32[8,1,192]{2,1,0:T(1,128)}), f32[8,1,192]{2,1,0:T(1,128)S(1)}, u32[]{:S(2)}, u32[]{:S(2)}) %all-to-all-start) | async-done | bytes 6176 | tf_op jit(solution)/shard_map/all_to_all | solution.py:11
  49.8 0.1 multiply_reduce_fusion.1
  49.9 0.7 broadcast_in_dim.11
  50.7 9.7 %all-to-all-start.1 = ((f32[32,2,768]{2,1,0:T(2,128)}), f32[32,2,768]{2,1,0:T(2,128)S(1)}, u32[]{:S(2)}, u32[]{:S(2)}) async-start(f32[32,2,768]{2,1,0:T(2,128)} %broadcast_in_dim.11), calls=%async_computation.1 | async-start | bytes 393216 | tf_op jit(solution)/shard_map/all_to_all | solution.py:11
  60.3 7.0 %collective-permute-start.1 = (f32[192,768]{1,0:T(8,128)S(1)}, f32[192,768]{1,0:T(8,128)S(1)}, u32[]{:S(2)}, u32[]{:S(2)}) collective-permute-start(f32[192,768]{1,0:T(8,128)S(1)} %get-tuple-element.28), channel_id=1, source_target_pairs={{0,256},{256,0},{1,257},{257,1},{2,258},{258,2},{3,259},{259,3},{4... | collective-permute-start | bytes 1769480 | tf_op jit(solution)/shard_map/ppermute | solution.py:25
  67.4 2.4 %all-to-all-done.1 = f32[32,2,768]{2,1,0:T(2,128)S(1)} async-done(((f32[32,2,768]{2,1,0:T(2,128)}), f32[32,2,768]{2,1,0:T(2,128)S(1)}, u32[]{:S(2)}, u32[]{:S(2)}) %all-to-all-start.1) | async-done | bytes 196640 | tf_op jit(solution)/shard_map/all_to_all | solution.py:11
  69.8 0.1 reduce_sum.139
  69.8 0.0 copy-done.2
  69.9 0.6 fusion.5
  70.5 0.6 divide_reduce_fusion
  71.1 1.4 pad_maximum_fusion.6
  72.4 13.8 %collective-permute-done.1 = f32[192,768]{1,0:T(8,128)S(1)} collective-permute-done((f32[192,768]{1,0:T(8,128)S(1)}, f32[192,768]{1,0:T(8,128)S(1)}, u32[]{:S(2)}, u32[]{:S(2)}) %collective-permute-start.1) | collective-permute-done | bytes 589856 | tf_op jit(solution)/shard_map/ppermute | solution.py:25
  86.3 0.2 add_reduce_fusion.1
  86.5 0.6 broadcast_in_dim.12
  87.1 10.2 %all-to-all-start.2 = ((f32[8,1,192]{2,1,0:T(1,128)}), f32[8,1,192]{2,1,0:T(1,128)S(1)}, u32[]{:S(2)}, u32[]{:S(2)}) async-start(f32[8,1,192]{2,1,0:T(1,128)} %broadcast_in_dim.12), calls=%async_computation.2 | async-start | bytes 16384 | tf_op jit(solution)/shard_map/all_to_all | solution.py:11
  97.3 4.9 %all-to-all-done.2 = f32[8,1,192]{2,1,0:T(1,128)S(1)} async-done(((f32[8,1,192]{2,1,0:T(1,128)}), f32[8,1,192]{2,1,0:T(1,128)S(1)}, u32[]{:S(2)}, u32[]{:S(2)}) %all-to-all-start.2) | async-done | bytes 6176 | tf_op jit(solution)/shard_map/all_to_all | solution.py:11
  102.3 0.1 multiply_reduce_fusion
  102.4 0.7 broadcast_in_dim.13
  103.2 9.2 %all-to-all-start.3 = ((f32[32,2,768]{2,1,0:T(2,128)}), f32[32,2,768]{2,1,0:T(2,128)S(1)}, u32[]{:S(2)}, u32[]{:S(2)}) async-start(f32[32,2,768]{2,1,0:T(2,128)} %broadcast_in_dim.13), calls=%async_computation.3 | async-start | bytes 393216 | tf_op jit(solution)/shard_map/all_to_all | solution.py:11
  112.4 0.6 pad_maximum_fusion.4
  113.0 8.8 %all-to-all-done.3 = f32[32,2,768]{2,1,0:T(2,128)S(1)} async-done(((f32[32,2,768]{2,1,0:T(2,128)}), f32[32,2,768]{2,1,0:T(2,128)S(1)}, u32[]{:S(2)}, u32[]{:S(2)}) %all-to-all-start.3) | async-done | bytes 196640 | tf_op jit(solution)/shard_map/all_to_all | solution.py:11
  121.8 0.1 reduce_sum.146
  121.9 0.6 rsqrt_reduce_fusion
  122.5 1.4 maximum_bitcast_fusion
  123.9 0.6 broadcast_in_dim.14
  124.5 6.1 %all-to-all-start.4 = ((f32[8,2,2]{2,1,0:T(2,128)}), f32[8,2,2]{2,1,0:T(2,128)S(1)}, u32[]{:S(2)}, u32[]{:S(2)}) async-start(f32[8,2,2]{2,1,0:T(2,128)} %broadcast_in_dim.14), calls=%async_computation.4 | async-start | bytes 16384 | tf_op jit(solution)/shard_map/all_to_all | solution.py:11
  130.6 0.6 pad_maximum_fusion.3
  131.2 4.3 %all-to-all-done.4 = f32[8,2,2]{2,1,0:T(2,128)S(1)} async-done(((f32[8,2,2]{2,1,0:T(2,128)}), f32[8,2,2]{2,1,0:T(2,128)S(1)}, u32[]{:S(2)}, u32[]{:S(2)}) %all-to-all-start.4) | async-done | bytes 160 | tf_op jit(solution)/shard_map/all_to_all | solution.py:11
  135.5 0.2 slice_reduce_fusion.1
  135.7 0.0 copy-start.4
  135.7 0.6 fusion.7
  136.3 1.3 rsqrt_multiply_fusion
  137.6 0.0 copy-start.1
  137.6 0.2 multiply_bitcast_fusion.1
  137.8 0.0 copy-done.4
  137.8 1.1 copy-done.1
  138.9 1.6 %multiply_subtract_fusion = (f32[2,192,768]{2,1,0:T(8,128)}, f32[2,192,768]{2,1,0:T(8,128)}) fusion(f32[2,192,768]{2,1,0:T(8,128)S(1)} %copy-done.1, f32[1,192,768]{2,1,0:T(8,128)S(1)} %get-tuple-element.26, f32[1,192,768]{2,1,0:T(8,128)S(1)} %get-tuple-element.25), kind=kLoop, calls=%fused_computation.1 | loop fusion | flops 884736 | bytes 4718592 | tf_op jit(solution)/shard_map/sub | solution.py:55
  (19 shorter events, 0.2 us)
Async XLA Ops:
  0.6 24.9 %copy-start = (bf16[1,4,192,768]{3,2,1,0:T(8,128)(2,1)S(1)}, bf16[1,4,192,768]{3,2,1,0:T(8,128)(2,1)}, u32[]{:S(2)}) copy-start(bf16[1,4,192,768]{3,2,1,0:T(8,128)(2,1)} %param.4) | copy-start | bytes 3538948
  0.6 44.2 %copy-start.3 = (f32[2,192]{1,0:T(2,128)S(1)}, f32[2,192]{1,0:T(2,128)}, u32[]{:S(2)}) copy-start(f32[2,192]{1,0:T(2,128)} %param.7) | copy-start | bytes 4612
  1.9 23.7 %collective-permute-start = (f32[192,768]{1,0:T(8,128)S(1)}, f32[192,768]{1,0:T(8,128)S(1)}, u32[]{:S(2)}, u32[]{:S(2)}) collective-permute-start(f32[192,768]{1,0:T(8,128)S(1)} %get-tuple-element.27), channel_id=1, source_target_pairs={{0,256},{256,0},{1,257},{257,1},{2,258},{258,2},{3,259},{259,3},{4... | collective-permute-start | bytes 1769480 | tf_op jit(solution)/shard_map/ppermute | solution.py:25
  13.4 56.5 %copy-start.2 = (f32[2,768]{1,0:T(2,128)S(1)}, f32[2,768]{1,0:T(2,128)}, u32[]{:S(2)}) copy-start(f32[2,768]{1,0:T(2,128)} %param.6) | copy-start | bytes 18436
  26.4 23.3 %all-to-all-start = ((f32[8,1,192]{2,1,0:T(1,128)}), f32[8,1,192]{2,1,0:T(1,128)S(1)}, u32[]{:S(2)}, u32[]{:S(2)}) async-start(f32[8,1,192]{2,1,0:T(1,128)} %broadcast_in_dim.10), calls=%async_computation | async-start | bytes 16384 | tf_op jit(solution)/shard_map/all_to_all | solution.py:11
  50.7 19.1 %all-to-all-start.1 = ((f32[32,2,768]{2,1,0:T(2,128)}), f32[32,2,768]{2,1,0:T(2,128)S(1)}, u32[]{:S(2)}, u32[]{:S(2)}) async-start(f32[32,2,768]{2,1,0:T(2,128)} %broadcast_in_dim.11), calls=%async_computation.1 | async-start | bytes 393216 | tf_op jit(solution)/shard_map/all_to_all | solution.py:11
  60.3 25.9 %collective-permute-start.1 = (f32[192,768]{1,0:T(8,128)S(1)}, f32[192,768]{1,0:T(8,128)S(1)}, u32[]{:S(2)}, u32[]{:S(2)}) collective-permute-start(f32[192,768]{1,0:T(8,128)S(1)} %get-tuple-element.28), channel_id=1, source_target_pairs={{0,256},{256,0},{1,257},{257,1},{2,258},{258,2},{3,259},{259,3},{4... | collective-permute-start | bytes 1769480 | tf_op jit(solution)/shard_map/ppermute | solution.py:25
  87.1 15.1 %all-to-all-start.2 = ((f32[8,1,192]{2,1,0:T(1,128)}), f32[8,1,192]{2,1,0:T(1,128)S(1)}, u32[]{:S(2)}, u32[]{:S(2)}) async-start(f32[8,1,192]{2,1,0:T(1,128)} %broadcast_in_dim.12), calls=%async_computation.2 | async-start | bytes 16384 | tf_op jit(solution)/shard_map/all_to_all | solution.py:11
  103.2 18.6 %all-to-all-start.3 = ((f32[32,2,768]{2,1,0:T(2,128)}), f32[32,2,768]{2,1,0:T(2,128)S(1)}, u32[]{:S(2)}, u32[]{:S(2)}) async-start(f32[32,2,768]{2,1,0:T(2,128)} %broadcast_in_dim.13), calls=%async_computation.3 | async-start | bytes 393216 | tf_op jit(solution)/shard_map/all_to_all | solution.py:11
  124.5 11.0 %all-to-all-start.4 = ((f32[8,2,2]{2,1,0:T(2,128)}), f32[8,2,2]{2,1,0:T(2,128)S(1)}, u32[]{:S(2)}, u32[]{:S(2)}) async-start(f32[8,2,2]{2,1,0:T(2,128)} %broadcast_in_dim.14), calls=%async_computation.4 | async-start | bytes 16384 | tf_op jit(solution)/shard_map/all_to_all | solution.py:11
  135.7 2.1 %copy-start.4 = (f32[2]{0:T(128)}, f32[2]{0:T(128)S(1)}, u32[]{:S(2)}) copy-start(f32[2]{0:T(128)S(1)} %get-tuple-element.21) | copy-start | bytes 28
  137.6 1.3 copy-start.1

commit v3 on v1

v3 whole, which is shorter than its diff:
```python
import jax
import jax.numpy as jnp
from jax import lax
from jax.sharding import PartitionSpec as P

D = 6144


def gather_sum(x, axis, size):
    copies = jnp.broadcast_to(x[None], (size,) + x.shape)
    return jnp.sum(lax.all_to_all(copies, axis, 0, 0, tiled=True), axis=0)


def per_device(n_row, n_col, grads, params, row_moments, col_moments):
    shares = grads[0]
    me = lax.axis_index("dp")
    width = jnp.float32(D)
    rows = row_moments.shape[1]

    def layer(first, k):
        return lax.dynamic_slice_in_dim(shares, first * 2 + k, 1, 0).astype(jnp.float32)

    def mean_in(old, total):
        return 0.8 * old + 0.2 * (total / width)

    got = [lax.ppermute(layer(1 - me, k), "dp", [(0, 1), (1, 0)]) for k in range(2)]

    def early(got0, rows_old):
        g = lax.optimization_barrier(layer(me, 0) + got0)
        square = g * g + 1e-30
        row_sum = gather_sum(jnp.sum(square, axis=1), "col", n_col)
        weighed = jnp.sum(g * g * (1.0 / mean_in(rows_old, row_sum))[:, None, :], axis=2)
        return g, row_sum, jnp.concatenate([jnp.sum(square, axis=2), weighed])

    def never(got0, rows_old):
        return got0, rows_old, got0[:, :, :2].reshape(2, -1)

    g0, row_sum0, cols0 = lax.cond(me < 2, early, never, got[0], row_moments[:1])
    got1, row_sum0, cols0 = lax.optimization_barrier((got[1], row_sum0, cols0))

    g1 = lax.optimization_barrier(layer(me, 1) + got1)
    square = g1 * g1 + 1e-30
    row_part = jnp.sum(square, axis=1)
    sums = gather_sum(jnp.concatenate([cols0[:1], jnp.sum(square, axis=2), cols0[1:], cols0[1:]], axis=0), "row", n_row)
    new_cols = mean_in(col_moments, sums[:2])
    weighed = jnp.sum(g1 * g1 * (1.0 / new_cols[1:])[:, :, None], axis=1)
    packed = jnp.concatenate([row_part, weighed, sums[2:3] / new_cols[:1]], axis=1)
    both = gather_sum(packed, "col", n_col)
    new_rows = mean_in(row_moments, jnp.concatenate([row_sum0, both[:, :rows]]))
    whole = jnp.pad(both[:, 2 * rows :] * (1.0 / n_row), ((0, 0), (0, 3 * rows - both.shape[1])))
    raw = jnp.concatenate([whole, both[:, rows : 2 * rows] / new_rows[1:]])
    tail = jnp.concatenate([jnp.sum(new_rows, axis=1), jnp.sum(raw, axis=1)])
    total = gather_sum(tail, "row", n_row)
    row_mean = total[:2] / width
    squares_sum = row_mean * total[2:]
    clip = jnp.maximum(jnp.float32(1.0), jnp.sqrt(squares_sum / (width * width)))
    scale = lax.rsqrt(new_cols) * (jnp.sqrt(row_mean) / clip)[:, None]
    grad = jnp.concatenate([g0, g1])
    update = grad * lax.rsqrt(new_rows)[:, None, :] * scale[:, :, None]
    return (params - 0.01 * update, update, new_rows, new_cols, row_mean)


def solution(mesh):
    n_row, n_col = mesh.shape["row"], mesh.shape["col"]
    return jax.shard_map(
        lambda *args: per_device(n_row, n_col, *args),
        mesh=mesh,
        in_specs=(
            P("dp", None, "col", "row"),
            P("dp", "col", "row"),
            P("dp", "row"),
            P("dp", "col"),
        ),
        out_specs=(
            P("dp", "col", "row"),
            P("dp", "col", "row"),
            P("dp", "row"),
            P("dp", "col"),
            P("dp"),
        ),
        check_vma=False,
    )
```

time: 111 us -> 109 us (0.982)
  waiting for transfers between devices: 24.9 us -> 10.3 us
  blocking collectives: 68 us -> 79 us
  starting transfers between devices: 11.5 us -> 13.4 us
    ppermute x1 -> x2, waiting for transfers between devices: 24.9 us -> 10.3 us  [per_device(): lax.ppermute(layer(1 - me, k), 'dp', [(0, 1), (1, 0)])]
    all_to_all x3 -> x4, blocking collectives: 68 us -> 79 us  [gather_sum(): return jnp.sum(lax.all_to_all(copies, axis, 0, 0, tiled=True), axis=0)]
    ppermute x1 -> x2, starting transfers between devices: 11.5 us -> 13.4 us  [per_device(): lax.ppermute(layer(1 - me, k), 'dp', [(0, 1), (1, 0)])]
    sub x1, other arithmetic: 2.95 us -> 1.64 us  [per_device(): return (params - 0.01 * update, update, new_rows, new_cols, row_mean)]
  transfers between devices with their start and end apart: 1 -> 2, of which waited for: 1 -> 1; matrix products, arithmetic and copies ran while one was open for 0% -> 0% of each run, Pallas kernels for 0% -> 0%
where the time goes in v3:
time: 109 us
  blocking collectives  79 us (72%)
  starting transfers between devices  13.4 us (12%)
  waiting for transfers between devices  10.3 us (9%)
  other arithmetic  4.84 us (4%)
    all_to_all x4, blocking collectives, gather_sum(): return jnp.sum(lax.all_to_all(copies, axis, 0, 0, tiled=True), axis=0)  79 us
    ppermute x2, starting transfers between devices, per_device(): lax.ppermute(layer(1 - me, k), 'dp', [(0, 1), (1, 0)])  13.4 us
    ppermute x2, waiting for transfers between devices, per_device(): lax.ppermute(layer(1 - me, k), 'dp', [(0, 1), (1, 0)])  10.3 us
  transfers between devices with their start and end apart: 2, of which 1 were waited for; matrix products, arithmetic and copies ran while one was open for 0% of the time, Pallas kernels for 0%

profile of v3, /device:TPU:1, one launch (start us, length us, event | category | flops | bytes accessed | tf_op | source)
XLA Modules:
  0.0 108.7 jit_solution(14596097451982949507)
XLA Ops:
  0.6 0.0 copy-start
  0.6 0.0 slice-start
  0.7 1.2 %bitcast_convert_fusion.1 = (f32[1,192,768]{2,1,0:T(8,128)S(1)}, f32[1,192,768]{2,1,0:T(8,128)S(1)}) fusion(bf16[1,4,192,768]{3,2,1,0:T(8,128)(2,1)} %param.6, s32[]{:T(128)S(6)} %select_n.12, s32[]{:T(128)S(6)} %select_n.14), kind=kLoop, calls=%fused_computation.14 | loop fusion | flops 294912 | bytes 1769480 | tf_op jit(solution)/shard_map/convert_element_type | solution.py:21
  1.9 11.5 %collective-permute-start = (f32[1,192,768]{2,1,0:T(8,128)S(1)}, f32[1,192,768]{2,1,0:T(8,128)S(1)}, u32[]{:S(2)}, u32[]{:S(2)}) collective-permute-start(f32[1,192,768]{2,1,0:T(8,128)S(1)} %get-tuple-element.46), channel_id=1, source_target_pairs={{0,256},{256,0},{1,257},{257,1},{2,258},{258,2},{3,259},{259,3},{4... | collective-permute-start | bytes 1769480 | tf_op jit(solution)/shard_map/ppermute | solution.py:26
  13.4 1.9 %collective-permute-start.1 = (f32[1,192,768]{2,1,0:T(8,128)S(1)}, f32[1,192,768]{2,1,0:T(8,128)S(1)}, u32[]{:S(2)}, u32[]{:S(2)}) collective-permute-start(f32[1,192,768]{2,1,0:T(8,128)S(1)} %get-tuple-element.47), channel_id=1, source_target_pairs={{0,256},{256,0},{1,257},{257,1},{2,258},{258,2},{3,259},{259,3},{4... | collective-permute-start | bytes 1769480 | tf_op jit(solution)/shard_map/ppermute | solution.py:26
  15.3 10.3 %collective-permute-done = f32[1,192,768]{2,1,0:T(8,128)S(1)} collective-permute-done((f32[1,192,768]{2,1,0:T(8,128)S(1)}, f32[1,192,768]{2,1,0:T(8,128)S(1)}, u32[]{:S(2)}, u32[]{:S(2)}) %collective-permute-start) | collective-permute-done | bytes 589856 | tf_op jit(solution)/shard_map/ppermute | solution.py:26
  25.6 0.0 copy-done
  25.6 0.0 slice-done
  25.6 20.1 %conditional.1 = (f32[1,192,768]{2,1,0:T(8,128)S(1)}, f32[1,768]{1,0:T(1,128)S(1)}, f32[2,192]{1,0:T(2,128)S(1)}) conditional(s32[]{:T(128)} %convert_element_type.59, (f32[1,192,768]{2,1,0:T(8,128)S(1)}, f32[1,768]{1,0:T(1,128)S(1)}) %tuple.32, (s32[]{:T(128)}, bf16[1,4,192,768]{3,2,1,0:T(8,128)(2,1)S(1)}, f32[1,192,768]{2,1,0:T(8,128)S(1)}, ...), branch_computations={%region_0.0_spmd, %region_1.0_spmd} | conditional | flops 1500676 | bytes 3079758 | solution.py:38
  25.6 0.1 convert_add_fusion
  25.7 0.1 add_reduce_fusion.1
  25.8 0.1 broadcast_in_dim.10
  25.8 19.5 %all_to_all.20 = f32[32,1,768]{2,1,0:T(1,128)S(1)} all-to-all(f32[32,1,768]{2,1,0:T(1,128)S(1)} %broadcast_in_dim.10), channel_id=1, replica_groups=mesh['dp'=2,'row'=8,'col'=32] {'col'}, dimensions={0} | all-to-all | bytes 196608 | tf_op jit(solution)/shard_map/cond/branch_1_fun/all_to_all | solution.py:11
  45.3 0.1 reduce_sum.68
  45.4 0.2 add_reduce_fusion
  45.6 0.0 copy-start.5
  45.7 0.0 collective-permute-done.1
  45.7 0.1 convert_add_fusion.1
  45.7 0.0 copy-start.3
  45.7 0.0 copy-start.1
  45.8 0.1 add_reduce_fusion.2
  45.9 36.4 %all_to_all.21 = f32[8,4,192]{2,1,0:T(4,128)S(1)} all-to-all(f32[8,4,192]{2,1,0:T(4,128)S(1)} %broadcast_in_dim.15), channel_id=1, replica_groups=mesh['dp'=2,'row'=8,'col'=32] {'row'}, dimensions={0} | all-to-all | bytes 49152 | tf_op jit(solution)/shard_map/all_to_all | solution.py:11
  82.4 0.0 copy-done.5
  82.4 0.0 copy-start.4
  82.5 0.1 add_reduce_fusion.3
  82.6 0.1 broadcast_in_dim.17
  82.8 12.6 %all_to_all.22 = f32[32,1,1728]{2,1,0:T(1,128)S(1)} all-to-all(f32[32,1,1728]{2,1,0:T(1,128)S(1)} %broadcast_in_dim.17), channel_id=1, replica_groups=mesh['dp'=2,'row'=8,'col'=32] {'col'}, dimensions={0} | all-to-all | bytes 442368 | tf_op jit(solution)/shard_map/all_to_all | solution.py:11
  95.4 0.1 reduce_sum.129
  95.6 0.0 copy-done.3
  95.6 0.0 copy-start.2
  95.6 0.1 reduce_sum.131
  95.8 0.1 fusion.3
  95.9 0.1 pad_maximum_fusion.2
  96.0 10.4 %all_to_all.23 = f32[8,1,4]{2,1,0:T(1,128)S(1)} all-to-all(f32[8,1,4]{2,1,0:T(1,128)S(1)} %broadcast_in_dim.18), channel_id=1, replica_groups=mesh['dp'=2,'row'=8,'col'=32] {'row'}, dimensions={0} | all-to-all | bytes 256 | tf_op jit(solution)/shard_map/all_to_all | solution.py:11
  106.4 0.5 maximum_divide_fusion
  106.9 0.1 rsqrt_multiply_fusion
  107.0 0.0 copy-done.1
  107.0 1.6 %multiply_subtract_fusion = (f32[2,192,768]{2,1,0:T(8,128)}, f32[2,192,768]{2,1,0:T(8,128)}) fusion(f32[2,192,768]{2,1,0:T(8,128)S(1)} %copy-done.1, f32[2,192]{1,0:T(2,128)S(1)} %rsqrt_multiply_fusion, f32[2,768]{1,0:T(2,128)S(1)} %get-tuple-element.42, f32[1,192,768]{2,1,0:T(8,128)S(1)} %convert_add_fusion.1, f32[1,192,768]{2,1,0:T(8,128)S(1)} %get-tuple-element.30), kind=kLoop, calls=%fused_computation.8 | loop fusion | flops 1474560 | bytes 4726272 | tf_op jit(solution)/shard_map/sub | solution.py:60
  108.6 0.0 copy-done.4
  108.7 0.0 copy-done.2
  (19 shorter events, 0.2 us)
Async XLA Ops:
  0.6 24.9 %copy-start = (bf16[1,4,192,768]{3,2,1,0:T(8,128)(2,1)S(1)}, bf16[1,4,192,768]{3,2,1,0:T(8,128)(2,1)}, u32[]{:S(2)}) copy-start(bf16[1,4,192,768]{3,2,1,0:T(8,128)(2,1)} %param.6) | copy-start | bytes 3538948
  0.6 24.9 %slice-start = ((f32[2,768]{1,0:T(2,128)}), f32[1,768]{1,0:T(1,128)S(1)}, s32[]{:S(2)}) async-start(f32[2,768]{1,0:T(2,128)} %param.8), calls=%async_computation.4 | async-start | bytes 6144 | tf_op jit(solution)/shard_map/slice | solution.py:38
  1.9 23.7 %collective-permute-start = (f32[1,192,768]{2,1,0:T(8,128)S(1)}, f32[1,192,768]{2,1,0:T(8,128)S(1)}, u32[]{:S(2)}, u32[]{:S(2)}) collective-permute-start(f32[1,192,768]{2,1,0:T(8,128)S(1)} %get-tuple-element.46), channel_id=1, source_target_pairs={{0,256},{256,0},{1,257},{257,1},{2,258},{258,2},{3,259},{259,3},{4... | collective-permute-start | bytes 1769480 | tf_op jit(solution)/shard_map/ppermute | solution.py:26
  13.4 32.3 %collective-permute-start.1 = (f32[1,192,768]{2,1,0:T(8,128)S(1)}, f32[1,192,768]{2,1,0:T(8,128)S(1)}, u32[]{:S(2)}, u32[]{:S(2)}) collective-permute-start(f32[1,192,768]{2,1,0:T(8,128)S(1)} %get-tuple-element.47), channel_id=1, source_target_pairs={{0,256},{256,0},{1,257},{257,1},{2,258},{258,2},{3,259},{259,3},{4... | collective-permute-start | bytes 1769480 | tf_op jit(solution)/shard_map/ppermute | solution.py:26
  45.6 36.8 %copy-start.5 = (f32[2,192]{1,0:T(2,128)S(1)}, f32[2,192]{1,0:T(2,128)}, u32[]{:S(2)}) copy-start(f32[2,192]{1,0:T(2,128)} %param.9) | copy-start | bytes 4612
  45.7 49.8 %copy-start.3 = (f32[2,768]{1,0:T(2,128)S(1)}, f32[2,768]{1,0:T(2,128)}, u32[]{:S(2)}) copy-start(f32[2,768]{1,0:T(2,128)} %param.8) | copy-start | bytes 18436
  45.7 61.3 %copy-start.1 = (f32[2,192,768]{2,1,0:T(8,128)S(1)}, f32[2,192,768]{2,1,0:T(8,128)}, u32[]{:S(2)}) copy-start(f32[2,192,768]{2,1,0:T(8,128)} %param.7) | copy-start | bytes 3538948
  82.4 26.2 %copy-start.4 = (f32[2,192]{1,0:T(2,128)}, f32[2,192]{1,0:T(2,128)S(1)}, u32[]{:S(2)}) copy-start(f32[2,192]{1,0:T(2,128)S(1)} %fusion.4) | copy-start | bytes 4612
  95.6 13.0 %copy-start.2 = (f32[2,768]{1,0:T(2,128)}, f32[2,768]{1,0:T(2,128)S(1)}, u32[]{:S(2)}) copy-start(f32[2,768]{1,0:T(2,128)S(1)} %get-tuple-element.43) | copy-start | bytes 18436

commit v4 on v3

--- a/solution.py
+++ b/solution.py
@@ -1,15 +1,78 @@
 import jax
 import jax.numpy as jnp
 from jax import lax
+from jax.experimental import pallas as pl
+from jax.experimental.pallas import tpu as pltpu
 from jax.sharding import PartitionSpec as P
 
 D = 6144
+PIECES = 2
 
 
 def gather_sum(x, axis, size):
     copies = jnp.broadcast_to(x[None], (size,) + x.shape)
     return jnp.sum(lax.all_to_all(copies, axis, 0, 0, tiled=True), axis=0)
 
+
+def finish_kernel(
+    tails_ref, g0_ref, g1_ref, params_ref, rows_ref, cols_ref,
+    new_params_ref, update_ref, row_mean_out, params_out, update_out, means, sems, mean_sem,
+):
+    width = jnp.float32(D)
+    total = jnp.sum(tails_ref[...], axis=0)
+    columns, rows = g0_ref.shape[1:]
+    step = columns // PIECES
+    for k in range(2):
+        means[k] = (total[:, k : k + 1] / width)[0, 0]
+    copies = [pltpu.make_async_copy(means, row_mean_out, mean_sem)]
+    copies[0].start()
+    for k, g_ref in enumerate((g0_ref, g1_ref)):
+        row_mean = total[:, k : k + 1] / width
+        squares_sum = row_mean * total[:, k + 2 : k + 3]
+        clip = jnp.maximum(jnp.float32(1.0), jnp.sqrt(squares_sum / (width * width)))
+        scale = lax.rsqrt(cols_ref[k : k + 1, :]) * (jnp.sqrt(row_mean) / clip)
+        scale = jnp.broadcast_to(scale, (128, columns)).T
+        per_row = lax.rsqrt(rows_ref[k : k + 1, :])
+        for p in range(PIECES):
+            part = pl.ds(p * step, step)
+            for q in range(rows // 128):
+                lanes = pl.ds(q * 128, 128)
+                update = (
+                    g_ref[0, part, lanes]
+                    * per_row[:, q * 128 : (q + 1) * 128]
+                    * scale[p * step : (p + 1) * step, :]
+                )
+                update_out[k, part, lanes] = update
+                params_out[k, part, lanes] = params_ref[k, part, lanes] - 0.01 * update
+            for n, (source, target) in enumerate(((update_out, update_ref), (params_out, new_params_ref))):
+                copy = pltpu.make_async_copy(source.at[k, part], target.at[k, part], sems.at[n, k * PIECES + p])
+                copy.start()
+                copies.append(copy)
+    for copy in copies:
+        copy.wait()
+
+
+def finish(tails, g0, g1, params, new_rows, new_cols):
+    whole = jax.ShapeDtypeStruct(params.shape, jnp.float32)
+    vmem = pl.BlockSpec(memory_space=pltpu.VMEM)
+    return pl.pallas_call(
+        finish_kernel,
+        out_shape=(whole, whole, jax.ShapeDtypeStruct((2,), jnp.float32)),
+        in_specs=[vmem] * 6,
+        out_specs=(
+            pl.BlockSpec(memory_space=pl.ANY),
+            pl.BlockSpec(memory_space=pl.ANY),
+            pl.BlockSpec(memory_space=pl.ANY),
+        ),
+        scratch_shapes=[
+            pltpu.VMEM(params.shape, jnp.float32),
+            pltpu.VMEM(params.shape, jnp.float32),
+            pltpu.SMEM((2,), jnp.float32),
+            pltpu.SemaphoreType.DMA((2, 2 * PIECES)),
+            pltpu.SemaphoreType.DMA,
+        ],
+        compiler_params=pltpu.CompilerParams(vmem_limit_bytes=16 << 20),
+    )(tails, g0, g1, params, new_rows, new_cols)
 
 def per_device(n_row, n_col, grads, params, row_moments, col_moments):
     shares = grads[0]
@@ -50,14 +113,10 @@
     whole = jnp.pad(both[:, 2 * rows :] * (1.0 / n_row), ((0, 0), (0, 3 * rows - both.shape[1])))
     raw = jnp.concatenate([whole, both[:, rows : 2 * rows] / new_rows[1:]])
     tail = jnp.concatenate([jnp.sum(new_rows, axis=1), jnp.sum(raw, axis=1)])
-    total = gather_sum(tail, "row", n_row)
-    row_mean = total[:2] / width
-    squares_sum = row_mean * total[2:]
-    clip = jnp.maximum(jnp.float32(1.0), jnp.sqrt(squares_sum / (width * width)))
-    scale = lax.rsqrt(new_cols) * (jnp.sqrt(row_mean) / clip)[:, None]
-    grad = jnp.concatenate([g0, g1])
-    update = grad * lax.rsqrt(new_rows)[:, None, :] * scale[:, :, None]
-    return (params - 0.01 * update, update, new_rows, new_cols, row_mean)
+    copies = jnp.broadcast_to(tail, (n_row, 1, 4))
+    tails = lax.all_to_all(copies, "row", 0, 0, tiled=True)
+    new_params, update, row_mean = finish(tails, g0, g1, params, new_rows, new_cols)
+    return (new_params, update, new_rows, new_cols, row_mean)
 
 
 def solution(mesh):

time: 109 us -> 108 us (level)
  other arithmetic: 4.84 us -> 2.6 us
  Pallas kernels: 0 us -> 1.75 us
    all_to_all x4 -> x3, blocking collectives: 79 us -> 68.6 us  [gather_sum(): return jnp.sum(lax.all_to_all(copies, axis, 0, 0, tiled=True), axis=0)]
    all_to_all x0 -> x1, blocking collectives: none -> 10.4 us  [per_device(): tails = lax.all_to_all(copies, 'row', 0, 0, tiled=True)]
    pallas_call x0 -> x1, Pallas kernels: none -> 1.75 us  [finish(): pl.pallas_call(finish_kernel, out_shape=(whole, whole, jax.ShapeDtypeStru...]
    sub x1 -> x0, other arithmetic: 1.64 us -> none  [per_device(): return (params - 0.01 * update, update, new_rows, new_cols, row_mean)]
  transfers between devices with their start and end apart: 2 -> 2, of which waited for: 1 -> 1; matrix products, arithmetic and copies ran while one was open for 0% -> 1% of each run, Pallas kernels for 0% -> 0%
where the time goes in v4:
time: 108 us
  blocking collectives  79 us (73%)
  starting transfers between devices  13.4 us (12%)
  waiting for transfers between devices  10.3 us (10%)
  other arithmetic  2.6 us (2%)
  Pallas kernels  1.75 us (2%)
    all_to_all x3, blocking collectives, gather_sum(): return jnp.sum(lax.all_to_all(copies, axis, 0, 0, tiled=True), axis=0)  68.6 us
    ppermute x2, starting transfers between devices, per_device(): lax.ppermute(layer(1 - me, k), 'dp', [(0, 1), (1, 0)])  13.4 us
    all_to_all x1, blocking collectives, per_device(): tails = lax.all_to_all(copies, 'row', 0, 0, tiled=True)  10.4 us
    ppermute x2, waiting for transfers between devices, per_device(): lax.ppermute(layer(1 - me, k), 'dp', [(0, 1), (1, 0)])  10.3 us
  transfers between devices with their start and end apart: 2, of which 1 were waited for; matrix products, arithmetic and copies ran while one was open for 1% of the time, Pallas kernels for 0%

profile of v4, /device:TPU:1, one launch (start us, length us, event | category | flops | bytes accessed | tf_op | source)
XLA Modules:
  0.0 108.1 jit_solution(9402207383387847021)
XLA Ops:
  0.6 0.0 copy-start.3
  0.6 0.0 slice-start
  0.7 1.2 %bitcast_convert_fusion = (f32[1,192,768]{2,1,0:T(8,128)S(1)}, f32[1,192,768]{2,1,0:T(8,128)S(1)}) fusion(bf16[1,4,192,768]{3,2,1,0:T(8,128)(2,1)} %param.6, s32[]{:T(128)S(6)} %select_n.13, s32[]{:T(128)S(6)} %select_n.12), kind=kLoop, calls=%fused_computation.10 | loop fusion | flops 294912 | bytes 1769480 | tf_op jit(solution)/shard_map/convert_element_type | solution.py:84
  1.9 11.5 %collective-permute-start.1 = (f32[1,192,768]{2,1,0:T(8,128)S(1)}, f32[1,192,768]{2,1,0:T(8,128)S(1)}, u32[]{:S(2)}, u32[]{:S(2)}) collective-permute-start(f32[1,192,768]{2,1,0:T(8,128)S(1)} %get-tuple-element.48), channel_id=1, source_target_pairs={{0,256},{256,0},{1,257},{257,1},{2,258},{258,2},{3,259},{259,3},{4... | collective-permute-start | bytes 1769480 | tf_op jit(solution)/shard_map/ppermute | solution.py:89
  13.4 1.9 %collective-permute-start = (f32[1,192,768]{2,1,0:T(8,128)S(1)}, f32[1,192,768]{2,1,0:T(8,128)S(1)}, u32[]{:S(2)}, u32[]{:S(2)}) collective-permute-start(f32[1,192,768]{2,1,0:T(8,128)S(1)} %get-tuple-element.49), channel_id=1, source_target_pairs={{0,256},{256,0},{1,257},{257,1},{2,258},{258,2},{3,259},{259,3},{4... | collective-permute-start | bytes 1769480 | tf_op jit(solution)/shard_map/ppermute | solution.py:89
  15.3 10.3 %collective-permute-done.1 = f32[1,192,768]{2,1,0:T(8,128)S(1)} collective-permute-done((f32[1,192,768]{2,1,0:T(8,128)S(1)}, f32[1,192,768]{2,1,0:T(8,128)S(1)}, u32[]{:S(2)}, u32[]{:S(2)}) %collective-permute-start.1) | collective-permute-done | bytes 589856 | tf_op jit(solution)/shard_map/ppermute | solution.py:89
  25.6 0.0 copy-done.3
  25.6 0.0 slice-done
  25.6 20.1 %conditional.1 = (f32[1,192,768]{2,1,0:T(8,128)S(1)}, f32[1,768]{1,0:T(1,128)S(1)}, f32[2,192]{1,0:T(2,128)S(1)}) conditional(s32[]{:T(128)} %convert_element_type.61, (f32[1,192,768]{2,1,0:T(8,128)S(1)}, f32[1,768]{1,0:T(1,128)S(1)}) %tuple.30, (s32[]{:T(128)}, bf16[1,4,192,768]{3,2,1,0:T(8,128)(2,1)S(1)}, f32[1,192,768]{2,1,0:T(8,128)S(1)}, ...), branch_computations={%region_0.0_spmd, %region_1.0_spmd} | conditional | flops 1500676 | bytes 3079758 | solution.py:101
  25.6 0.1 convert_add_fusion
  25.7 0.1 add_reduce_fusion.1
  25.8 0.1 broadcast_in_dim.10
  25.8 19.5 %all_to_all.19 = f32[32,1,768]{2,1,0:T(1,128)S(1)} all-to-all(f32[32,1,768]{2,1,0:T(1,128)S(1)} %broadcast_in_dim.10), channel_id=1, replica_groups=mesh['dp'=2,'row'=8,'col'=32] {'col'}, dimensions={0} | all-to-all | bytes 196608 | tf_op jit(solution)/shard_map/cond/branch_1_fun/all_to_all | solution.py:14
  45.3 0.1 reduce_sum.67
  45.4 0.2 add_reduce_fusion
  45.6 0.0 copy-start.5
  45.7 0.0 collective-permute-done
  45.7 0.1 convert_add_fusion.1.g1_ref
  45.7 0.0 copy-start.4
  45.8 0.0 copy-start
  45.8 0.1 add_reduce_fusion.2
  45.9 36.4 %all_to_all.20 = f32[8,4,192]{2,1,0:T(4,128)S(1)} all-to-all(f32[8,4,192]{2,1,0:T(4,128)S(1)} %broadcast_in_dim.15), channel_id=1, replica_groups=mesh['dp'=2,'row'=8,'col'=32] {'row'}, dimensions={0} | all-to-all | bytes 49152 | tf_op jit(solution)/shard_map/all_to_all | solution.py:14
  82.4 0.0 copy-done.5
  82.4 0.0 copy-start.2
  82.5 0.1 add_reduce_fusion.3
  82.6 0.1 broadcast_in_dim.17
  82.8 12.6 %all_to_all.21 = f32[32,1,1728]{2,1,0:T(1,128)S(1)} all-to-all(f32[32,1,1728]{2,1,0:T(1,128)S(1)} %broadcast_in_dim.17), channel_id=1, replica_groups=mesh['dp'=2,'row'=8,'col'=32] {'col'}, dimensions={0} | all-to-all | bytes 442368 | tf_op jit(solution)/shard_map/all_to_all | solution.py:14
  95.4 0.1 reduce_sum.120
  95.6 0.0 copy-done.4
  95.6 0.1 fusion.4
  95.7 0.0 copy-start.1
  95.7 0.1 fusion.2
  95.9 0.1 pad_maximum_fusion.2
  95.9 10.4 %all_to_all.22.tails_ref = f32[8,1,4]{2,1,0:T(1,128)S(1)} all-to-all(f32[8,1,4]{2,1,0:T(1,128)S(1)} %broadcast_in_dim.18), channel_id=1, replica_groups=mesh['dp'=2,'row'=8,'col'=32] {'row'}, dimensions={0} | all-to-all | bytes 256 | tf_op jit(solution)/shard_map/all_to_all | solution.py:117
  106.4 0.0 copy-done
  106.4 1.8 %shard_map.83 = (f32[2,192,768]{2,1,0:T(8,128)}, f32[2,192,768]{2,1,0:T(8,128)}, f32[2]{0:T(128)}) custom-call(f32[8,1,4]{2,1,0:T(1,128)S(1)} %all_to_all.22.tails_ref, f32[1,192,768]{2,1,0:T(8,128)S(1)} %get-tuple-element.38.g0_ref, f32[1,192,768]{2,1,0:T(8,128)S(1)} %convert_add_fusion.1.g1_ref, f32[2,192,768]{2,1,0:T(8,128)S(1)} %copy-done, ...), custom_call_target="tpu_custom_call" | custom-call | tf_op jit(solution)/shard_map/pallas_call | solution.py:58
  108.1 0.0 copy-done.2
  108.1 0.0 copy-done.1
  (17 shorter events, 0.2 us)
Async XLA Ops:
  0.6 24.9 %copy-start.3 = (bf16[1,4,192,768]{3,2,1,0:T(8,128)(2,1)S(1)}, bf16[1,4,192,768]{3,2,1,0:T(8,128)(2,1)}, u32[]{:S(2)}) copy-start(bf16[1,4,192,768]{3,2,1,0:T(8,128)(2,1)} %param.6) | copy-start | bytes 3538948
  0.6 24.9 %slice-start = ((f32[2,768]{1,0:T(2,128)}), f32[1,768]{1,0:T(1,128)S(1)}, s32[]{:S(2)}) async-start(f32[2,768]{1,0:T(2,128)} %param.8), calls=%async_computation.4 | async-start | bytes 6144 | tf_op jit(solution)/shard_map/slice | solution.py:101
  1.9 23.7 %collective-permute-start.1 = (f32[1,192,768]{2,1,0:T(8,128)S(1)}, f32[1,192,768]{2,1,0:T(8,128)S(1)}, u32[]{:S(2)}, u32[]{:S(2)}) collective-permute-start(f32[1,192,768]{2,1,0:T(8,128)S(1)} %get-tuple-element.48), channel_id=1, source_target_pairs={{0,256},{256,0},{1,257},{257,1},{2,258},{258,2},{3,259},{259,3},{4... | collective-permute-start | bytes 1769480 | tf_op jit(solution)/shard_map/ppermute | solution.py:89
  13.4 32.3 %collective-permute-start = (f32[1,192,768]{2,1,0:T(8,128)S(1)}, f32[1,192,768]{2,1,0:T(8,128)S(1)}, u32[]{:S(2)}, u32[]{:S(2)}) collective-permute-start(f32[1,192,768]{2,1,0:T(8,128)S(1)} %get-tuple-element.49), channel_id=1, source_target_pairs={{0,256},{256,0},{1,257},{257,1},{2,258},{258,2},{3,259},{259,3},{4... | collective-permute-start | bytes 1769480 | tf_op jit(solution)/shard_map/ppermute | solution.py:89
  45.6 36.8 %copy-start.5 = (f32[2,192]{1,0:T(2,128)S(1)}, f32[2,192]{1,0:T(2,128)}, u32[]{:S(2)}) copy-start(f32[2,192]{1,0:T(2,128)} %param.9) | copy-start | bytes 4612
  45.7 49.8 %copy-start.4 = (f32[2,768]{1,0:T(2,128)S(1)}, f32[2,768]{1,0:T(2,128)}, u32[]{:S(2)}) copy-start(f32[2,768]{1,0:T(2,128)} %param.8) | copy-start | bytes 18436
  45.8 60.6 %copy-start = (f32[2,192,768]{2,1,0:T(8,128)S(1)}, f32[2,192,768]{2,1,0:T(8,128)}, u32[]{:S(2)}) copy-start(f32[2,192,768]{2,1,0:T(8,128)} %params_ref.1) | copy-start | bytes 3538948
  82.4 25.7 %copy-start.2 = (f32[2,192]{1,0:T(2,128)}, f32[2,192]{1,0:T(2,128)S(1)}, u32[]{:S(2)}) copy-start(f32[2,192]{1,0:T(2,128)S(1)} %fusion.3.cols_ref) | copy-start | bytes 4612
  95.7 12.4 %copy-start.1 = (f32[2,768]{1,0:T(2,128)}, f32[2,768]{1,0:T(2,128)S(1)}, u32[]{:S(2)}) copy-start(f32[2,768]{1,0:T(2,128)S(1)} %get-tuple-element.47.rows_ref) | copy-start | bytes 18436

commit v5 on v4

--- a/solution.py
+++ b/solution.py
@@ -107,11 +107,19 @@
     sums = gather_sum(jnp.concatenate([cols0[:1], jnp.sum(square, axis=2), cols0[1:], cols0[1:]], axis=0), "row", n_row)
     new_cols = mean_in(col_moments, sums[:2])
     weighed = jnp.sum(g1 * g1 * (1.0 / new_cols[1:])[:, :, None], axis=1)
-    packed = jnp.concatenate([row_part, weighed, sums[2:3] / new_cols[:1]], axis=1)
+    share = sums[2:3] / new_cols[:1]
+    cut = share.shape[1] // 2
+    packed = jnp.concatenate(
+        [
+            jnp.concatenate([row_part, share[:, :cut]], axis=1),
+            jnp.concatenate([weighed, share[:, cut:]], axis=1),
+        ]
+    )
     both = gather_sum(packed, "col", n_col)
-    new_rows = mean_in(row_moments, jnp.concatenate([row_sum0, both[:, :rows]]))
-    whole = jnp.pad(both[:, 2 * rows :] * (1.0 / n_row), ((0, 0), (0, 3 * rows - both.shape[1])))
-    raw = jnp.concatenate([whole, both[:, rows : 2 * rows] / new_rows[1:]])
+    new_rows = mean_in(row_moments, jnp.concatenate([row_sum0, both[:1, :rows]]))
+    whole = (both[:1, rows:] + both[1:, rows:]) * (1.0 / n_row)
+    whole = jnp.pad(whole, ((0, 0), (0, rows - whole.shape[1])))
+    raw = jnp.concatenate([whole, both[1:, :rows] / new_rows[1:]])
     tail = jnp.concatenate([jnp.sum(new_rows, axis=1), jnp.sum(raw, axis=1)])
     copies = jnp.broadcast_to(tail, (n_row, 1, 4))
     tails = lax.all_to_all(copies, "row", 0, 0, tiled=True)

time: 108 us -> 108 us (level)
  no operation moved by 1% of the time
where the time goes in v5:
time: 108 us
  blocking collectives  79 us (73%)
  starting transfers between devices  13.4 us (12%)
  waiting for transfers between devices  10.3 us (10%)
  other arithmetic  2.53 us (2%)
  Pallas kernels  1.75 us (2%)
    all_to_all x3, blocking collectives, gather_sum(): return jnp.sum(lax.all_to_all(copies, axis, 0, 0, tiled=True), axis=0)  68.6 us
    ppermute x2, starting transfers between devices, per_device(): lax.ppermute(layer(1 - me, k), 'dp', [(0, 1), (1, 0)])  13.4 us
    all_to_all x1, blocking collectives, per_device(): tails = lax.all_to_all(copies, 'row', 0, 0, tiled=True)  10.4 us
    ppermute x2, waiting for transfers between devices, per_device(): lax.ppermute(layer(1 - me, k), 'dp', [(0, 1), (1, 0)])  10.3 us
  transfers between devices with their start and end apart: 2, of which 1 were waited for; matrix products, arithmetic and copies ran while one was open for 1% of the time, Pallas kernels for 0%

profile of v5, /device:TPU:1, one launch (start us, length us, event | category | flops | bytes accessed | tf_op | source)
XLA Modules:
  0.0 108.1 jit_solution(11947882293697635394)
XLA Ops:
  0.6 0.0 copy-start.3
  0.6 0.0 slice-start
  0.7 1.2 %bitcast_convert_fusion = (f32[1,192,768]{2,1,0:T(8,128)S(1)}, f32[1,192,768]{2,1,0:T(8,128)S(1)}) fusion(bf16[1,4,192,768]{3,2,1,0:T(8,128)(2,1)} %param.6, s32[]{:T(128)S(6)} %select_n.13, s32[]{:T(128)S(6)} %select_n.12), kind=kLoop, calls=%fused_computation.10 | loop fusion | flops 294912 | bytes 1769480 | tf_op jit(solution)/shard_map/convert_element_type | solution.py:84
  1.9 11.5 %collective-permute-start.1 = (f32[1,192,768]{2,1,0:T(8,128)S(1)}, f32[1,192,768]{2,1,0:T(8,128)S(1)}, u32[]{:S(2)}, u32[]{:S(2)}) collective-permute-start(f32[1,192,768]{2,1,0:T(8,128)S(1)} %get-tuple-element.48), channel_id=1, source_target_pairs={{0,256},{256,0},{1,257},{257,1},{2,258},{258,2},{3,259},{259,3},{4... | collective-permute-start | bytes 1769480 | tf_op jit(solution)/shard_map/ppermute | solution.py:89
  13.4 1.9 %collective-permute-start = (f32[1,192,768]{2,1,0:T(8,128)S(1)}, f32[1,192,768]{2,1,0:T(8,128)S(1)}, u32[]{:S(2)}, u32[]{:S(2)}) collective-permute-start(f32[1,192,768]{2,1,0:T(8,128)S(1)} %get-tuple-element.49), channel_id=1, source_target_pairs={{0,256},{256,0},{1,257},{257,1},{2,258},{258,2},{3,259},{259,3},{4... | collective-permute-start | bytes 1769480 | tf_op jit(solution)/shard_map/ppermute | solution.py:89
  15.3 10.3 %collective-permute-done.1 = f32[1,192,768]{2,1,0:T(8,128)S(1)} collective-permute-done((f32[1,192,768]{2,1,0:T(8,128)S(1)}, f32[1,192,768]{2,1,0:T(8,128)S(1)}, u32[]{:S(2)}, u32[]{:S(2)}) %collective-permute-start.1) | collective-permute-done | bytes 589856 | tf_op jit(solution)/shard_map/ppermute | solution.py:89
  25.6 0.0 copy-done.3
  25.6 0.0 slice-done
  25.6 20.1 %conditional.1 = (f32[1,192,768]{2,1,0:T(8,128)S(1)}, f32[1,768]{1,0:T(1,128)S(1)}, f32[2,192]{1,0:T(2,128)S(1)}) conditional(s32[]{:T(128)} %convert_element_type.61, (f32[1,192,768]{2,1,0:T(8,128)S(1)}, f32[1,768]{1,0:T(1,128)S(1)}) %tuple.31, (s32[]{:T(128)}, bf16[1,4,192,768]{3,2,1,0:T(8,128)(2,1)S(1)}, f32[1,192,768]{2,1,0:T(8,128)S(1)}, ...), branch_computations={%region_0.0_spmd, %region_1.0_spmd} | conditional | flops 1500676 | bytes 3079758 | solution.py:101
  25.6 0.1 convert_add_fusion
  25.7 0.1 add_reduce_fusion.1
  25.8 0.1 broadcast_in_dim.4
  25.8 19.5 %all_to_all.19 = f32[32,1,768]{2,1,0:T(1,128)S(1)} all-to-all(f32[32,1,768]{2,1,0:T(1,128)S(1)} %broadcast_in_dim.4), channel_id=1, replica_groups=mesh['dp'=2,'row'=8,'col'=32] {'col'}, dimensions={0} | all-to-all | bytes 196608 | tf_op jit(solution)/shard_map/cond/branch_1_fun/all_to_all | solution.py:14
  45.3 0.1 reduce_sum.68
  45.4 0.2 add_reduce_fusion
  45.6 0.0 copy-start.5
  45.7 0.0 collective-permute-done
  45.7 0.1 convert_add_fusion.1.g1_ref
  45.7 0.0 copy-start.4
  45.8 0.0 copy-start
  45.8 0.1 add_reduce_fusion.2
  45.9 36.4 %all_to_all.20 = f32[8,4,192]{2,1,0:T(4,128)S(1)} all-to-all(f32[8,4,192]{2,1,0:T(4,128)S(1)} %broadcast_in_dim.13), channel_id=1, replica_groups=mesh['dp'=2,'row'=8,'col'=32] {'row'}, dimensions={0} | all-to-all | bytes 49152 | tf_op jit(solution)/shard_map/all_to_all | solution.py:14
  82.4 0.0 copy-done.5
  82.4 0.0 copy-start.2
  82.5 0.1 fusion.8
  82.5 0.1 add_reduce_fusion.3
  82.7 0.1 broadcast_in_dim.14
  82.8 12.6 %all_to_all.21 = f32[32,2,864]{2,1,0:T(2,128)S(1)} all-to-all(f32[32,2,864]{2,1,0:T(2,128)S(1)} %broadcast_in_dim.14), channel_id=1, replica_groups=mesh['dp'=2,'row'=8,'col'=32] {'col'}, dimensions={0} | all-to-all | bytes 442368 | tf_op jit(solution)/shard_map/all_to_all | solution.py:14
  95.4 0.1 reduce_sum.118
  95.5 0.0 copy-done.4
  95.5 0.1 fusion.5
  95.6 0.0 copy-start.1
  95.7 0.1 fusion.2
  95.8 0.1 pad_maximum_fusion.2
  95.9 10.4 %all_to_all.22.tails_ref = f32[8,1,4]{2,1,0:T(1,128)S(1)} all-to-all(f32[8,1,4]{2,1,0:T(1,128)S(1)} %broadcast_in_dim.15), channel_id=1, replica_groups=mesh['dp'=2,'row'=8,'col'=32] {'row'}, dimensions={0} | all-to-all | bytes 256 | tf_op jit(solution)/shard_map/all_to_all | solution.py:125
  106.3 0.0 copy-done
  106.3 1.8 %shard_map.83 = (f32[2,192,768]{2,1,0:T(8,128)}, f32[2,192,768]{2,1,0:T(8,128)}, f32[2]{0:T(128)}) custom-call(f32[8,1,4]{2,1,0:T(1,128)S(1)} %all_to_all.22.tails_ref, f32[1,192,768]{2,1,0:T(8,128)S(1)} %get-tuple-element.38.g0_ref, f32[1,192,768]{2,1,0:T(8,128)S(1)} %convert_add_fusion.1.g1_ref, f32[2,192,768]{2,1,0:T(8,128)S(1)} %copy-done, ...), custom_call_target="tpu_custom_call" | custom-call | tf_op jit(solution)/shard_map/pallas_call | solution.py:58
  108.1 0.0 copy-done.2
  108.1 0.0 copy-done.1
  (16 shorter events, 0.2 us)
Async XLA Ops:
  0.6 24.9 %copy-start.3 = (bf16[1,4,192,768]{3,2,1,0:T(8,128)(2,1)S(1)}, bf16[1,4,192,768]{3,2,1,0:T(8,128)(2,1)}, u32[]{:S(2)}) copy-start(bf16[1,4,192,768]{3,2,1,0:T(8,128)(2,1)} %param.6) | copy-start | bytes 3538948
  0.6 24.9 %slice-start = ((f32[2,768]{1,0:T(2,128)}), f32[1,768]{1,0:T(1,128)S(1)}, s32[]{:S(2)}) async-start(f32[2,768]{1,0:T(2,128)} %param.8), calls=%async_computation.4 | async-start | bytes 6144 | tf_op jit(solution)/shard_map/slice | solution.py:101
  1.9 23.7 %collective-permute-start.1 = (f32[1,192,768]{2,1,0:T(8,128)S(1)}, f32[1,192,768]{2,1,0:T(8,128)S(1)}, u32[]{:S(2)}, u32[]{:S(2)}) collective-permute-start(f32[1,192,768]{2,1,0:T(8,128)S(1)} %get-tuple-element.48), channel_id=1, source_target_pairs={{0,256},{256,0},{1,257},{257,1},{2,258},{258,2},{3,259},{259,3},{4... | collective-permute-start | bytes 1769480 | tf_op jit(solution)/shard_map/ppermute | solution.py:89
  13.4 32.3 %collective-permute-start = (f32[1,192,768]{2,1,0:T(8,128)S(1)}, f32[1,192,768]{2,1,0:T(8,128)S(1)}, u32[]{:S(2)}, u32[]{:S(2)}) collective-permute-start(f32[1,192,768]{2,1,0:T(8,128)S(1)} %get-tuple-element.49), channel_id=1, source_target_pairs={{0,256},{256,0},{1,257},{257,1},{2,258},{258,2},{3,259},{259,3},{4... | collective-permute-start | bytes 1769480 | tf_op jit(solution)/shard_map/ppermute | solution.py:89
  45.6 36.8 %copy-start.5 = (f32[2,192]{1,0:T(2,128)S(1)}, f32[2,192]{1,0:T(2,128)}, u32[]{:S(2)}) copy-start(f32[2,192]{1,0:T(2,128)} %param.9) | copy-start | bytes 4612
  45.7 49.8 %copy-start.4 = (f32[2,768]{1,0:T(2,128)S(1)}, f32[2,768]{1,0:T(2,128)}, u32[]{:S(2)}) copy-start(f32[2,768]{1,0:T(2,128)} %param.8) | copy-start | bytes 18436
  45.8 60.5 %copy-start = (f32[2,192,768]{2,1,0:T(8,128)S(1)}, f32[2,192,768]{2,1,0:T(8,128)}, u32[]{:S(2)}) copy-start(f32[2,192,768]{2,1,0:T(8,128)} %params_ref.1) | copy-start | bytes 3538948
  82.4 25.6 %copy-start.2 = (f32[2,192]{1,0:T(2,128)}, f32[2,192]{1,0:T(2,128)S(1)}, u32[]{:S(2)}) copy-start(f32[2,192]{1,0:T(2,128)S(1)} %fusion.3.cols_ref) | copy-start | bytes 4612
  95.6 12.4 %copy-start.1 = (f32[2,768]{1,0:T(2,128)}, f32[2,768]{1,0:T(2,128)S(1)}, u32[]{:S(2)}) copy-start(f32[2,768]{1,0:T(2,128)S(1)} %get-tuple-element.47.rows_ref) | copy-start | bytes 18436

commit v6 on v4

--- a/solution.py
+++ b/solution.py
@@ -104,7 +104,7 @@
     g1 = lax.optimization_barrier(layer(me, 1) + got1)
     square = g1 * g1 + 1e-30
     row_part = jnp.sum(square, axis=1)
-    sums = gather_sum(jnp.concatenate([cols0[:1], jnp.sum(square, axis=2), cols0[1:], cols0[1:]], axis=0), "row", n_row)
+    sums = gather_sum(jnp.concatenate([cols0[:1], jnp.sum(square, axis=2), cols0[1:]], axis=0), "row", n_row)
     new_cols = mean_in(col_moments, sums[:2])
     weighed = jnp.sum(g1 * g1 * (1.0 / new_cols[1:])[:, :, None], axis=1)
     packed = jnp.concatenate([row_part, weighed, sums[2:3] / new_cols[:1]], axis=1)

time: 108 us -> 108 us (level)
  no operation moved by 1% of the time
where the time goes in v6:
time: 108 us
  blocking collectives  79 us (73%)
  starting transfers between devices  13.4 us (12%)
  waiting for transfers between devices  10.3 us (10%)
  other arithmetic  2.6 us (2%)
  Pallas kernels  1.75 us (2%)
    all_to_all x3, blocking collectives, gather_sum(): return jnp.sum(lax.all_to_all(copies, axis, 0, 0, tiled=True), axis=0)  68.6 us
    ppermute x2, starting transfers between devices, per_device(): lax.ppermute(layer(1 - me, k), 'dp', [(0, 1), (1, 0)])  13.4 us
    all_to_all x1, blocking collectives, per_device(): tails = lax.all_to_all(copies, 'row', 0, 0, tiled=True)  10.4 us
    ppermute x2, waiting for transfers between devices, per_device(): lax.ppermute(layer(1 - me, k), 'dp', [(0, 1), (1, 0)])  10.3 us
  transfers between devices with their start and end apart: 2, of which 1 were waited for; matrix products, arithmetic and copies ran while one was open for 1% of the time, Pallas kernels for 0%

profile of v6, /device:TPU:1, one launch (start us, length us, event | category | flops | bytes accessed | tf_op | source)
XLA Modules:
  0.0 108.1 jit_solution(646857862681600611)
XLA Ops:
  0.6 0.0 copy-start.3
  0.6 0.0 slice-start
  0.7 1.2 %bitcast_convert_fusion = (f32[1,192,768]{2,1,0:T(8,128)S(1)}, f32[1,192,768]{2,1,0:T(8,128)S(1)}) fusion(bf16[1,4,192,768]{3,2,1,0:T(8,128)(2,1)} %param.6, s32[]{:T(128)S(6)} %select_n.13, s32[]{:T(128)S(6)} %select_n.12), kind=kLoop, calls=%fused_computation.10 | loop fusion | flops 294912 | bytes 1769480 | tf_op jit(solution)/shard_map/convert_element_type | solution.py:84
  1.9 11.5 %collective-permute-start.1 = (f32[1,192,768]{2,1,0:T(8,128)S(1)}, f32[1,192,768]{2,1,0:T(8,128)S(1)}, u32[]{:S(2)}, u32[]{:S(2)}) collective-permute-start(f32[1,192,768]{2,1,0:T(8,128)S(1)} %get-tuple-element.48), channel_id=1, source_target_pairs={{0,256},{256,0},{1,257},{257,1},{2,258},{258,2},{3,259},{259,3},{4... | collective-permute-start | bytes 1769480 | tf_op jit(solution)/shard_map/ppermute | solution.py:89
  13.4 1.9 %collective-permute-start = (f32[1,192,768]{2,1,0:T(8,128)S(1)}, f32[1,192,768]{2,1,0:T(8,128)S(1)}, u32[]{:S(2)}, u32[]{:S(2)}) collective-permute-start(f32[1,192,768]{2,1,0:T(8,128)S(1)} %get-tuple-element.49), channel_id=1, source_target_pairs={{0,256},{256,0},{1,257},{257,1},{2,258},{258,2},{3,259},{259,3},{4... | collective-permute-start | bytes 1769480 | tf_op jit(solution)/shard_map/ppermute | solution.py:89
  15.3 10.3 %collective-permute-done.1 = f32[1,192,768]{2,1,0:T(8,128)S(1)} collective-permute-done((f32[1,192,768]{2,1,0:T(8,128)S(1)}, f32[1,192,768]{2,1,0:T(8,128)S(1)}, u32[]{:S(2)}, u32[]{:S(2)}) %collective-permute-start.1) | collective-permute-done | bytes 589856 | tf_op jit(solution)/shard_map/ppermute | solution.py:89
  25.6 0.0 copy-done.3
  25.6 0.0 slice-done
  25.6 20.1 %conditional.1 = (f32[1,192,768]{2,1,0:T(8,128)S(1)}, f32[1,768]{1,0:T(1,128)S(1)}, f32[2,192]{1,0:T(2,128)S(1)}) conditional(s32[]{:T(128)} %convert_element_type.61, (f32[1,192,768]{2,1,0:T(8,128)S(1)}, f32[1,768]{1,0:T(1,128)S(1)}) %tuple.30, (s32[]{:T(128)}, bf16[1,4,192,768]{3,2,1,0:T(8,128)(2,1)S(1)}, f32[1,192,768]{2,1,0:T(8,128)S(1)}, ...), branch_computations={%region_0.0_spmd, %region_1.0_spmd} | conditional | flops 1500676 | bytes 3079758 | solution.py:101
  25.6 0.1 convert_add_fusion
  25.7 0.1 add_reduce_fusion.1
  25.8 0.1 broadcast_in_dim.10
  25.8 19.5 %all_to_all.19 = f32[32,1,768]{2,1,0:T(1,128)S(1)} all-to-all(f32[32,1,768]{2,1,0:T(1,128)S(1)} %broadcast_in_dim.10), channel_id=1, replica_groups=mesh['dp'=2,'row'=8,'col'=32] {'col'}, dimensions={0} | all-to-all | bytes 196608 | tf_op jit(solution)/shard_map/cond/branch_1_fun/all_to_all | solution.py:14
  45.3 0.1 reduce_sum.67
  45.4 0.2 add_reduce_fusion
  45.6 0.0 copy-start.5
  45.7 0.0 collective-permute-done
  45.7 0.1 convert_add_fusion.1.g1_ref
  45.7 0.0 copy-start.4
  45.8 0.0 copy-start
  45.8 0.1 add_reduce_fusion.2
  45.9 36.4 %all_to_all.20 = f32[8,3,192]{2,1,0:T(4,128)S(1)} all-to-all(f32[8,3,192]{2,1,0:T(4,128)S(1)} %broadcast_in_dim.15), channel_id=1, replica_groups=mesh['dp'=2,'row'=8,'col'=32] {'row'}, dimensions={0} | all-to-all | bytes 36864 | tf_op jit(solution)/shard_map/all_to_all | solution.py:14
  82.4 0.0 copy-done.5
  82.4 0.0 copy-start.2
  82.5 0.1 add_reduce_fusion.3
  82.6 0.1 broadcast_in_dim.17
  82.8 12.6 %all_to_all.21 = f32[32,1,1728]{2,1,0:T(1,128)S(1)} all-to-all(f32[32,1,1728]{2,1,0:T(1,128)S(1)} %broadcast_in_dim.17), channel_id=1, replica_groups=mesh['dp'=2,'row'=8,'col'=32] {'col'}, dimensions={0} | all-to-all | bytes 442368 | tf_op jit(solution)/shard_map/all_to_all | solution.py:14
  95.4 0.1 reduce_sum.120
  95.6 0.0 copy-done.4
  95.6 0.1 fusion.4
  95.7 0.0 copy-start.1
  95.7 0.1 fusion.2
  95.9 0.1 pad_maximum_fusion.2
  95.9 10.4 %all_to_all.22.tails_ref = f32[8,1,4]{2,1,0:T(1,128)S(1)} all-to-all(f32[8,1,4]{2,1,0:T(1,128)S(1)} %broadcast_in_dim.18), channel_id=1, replica_groups=mesh['dp'=2,'row'=8,'col'=32] {'row'}, dimensions={0} | all-to-all | bytes 256 | tf_op jit(solution)/shard_map/all_to_all | solution.py:117
  106.4 0.0 copy-done
  106.4 1.8 %shard_map.83 = (f32[2,192,768]{2,1,0:T(8,128)}, f32[2,192,768]{2,1,0:T(8,128)}, f32[2]{0:T(128)}) custom-call(f32[8,1,4]{2,1,0:T(1,128)S(1)} %all_to_all.22.tails_ref, f32[1,192,768]{2,1,0:T(8,128)S(1)} %get-tuple-element.38.g0_ref, f32[1,192,768]{2,1,0:T(8,128)S(1)} %convert_add_fusion.1.g1_ref, f32[2,192,768]{2,1,0:T(8,128)S(1)} %copy-done, ...), custom_call_target="tpu_custom_call" | custom-call | tf_op jit(solution)/shard_map/pallas_call | solution.py:58
  108.1 0.0 copy-done.2
  108.1 0.0 copy-done.1
  (17 shorter events, 0.2 us)
Async XLA Ops:
  0.6 24.9 %copy-start.3 = (bf16[1,4,192,768]{3,2,1,0:T(8,128)(2,1)S(1)}, bf16[1,4,192,768]{3,2,1,0:T(8,128)(2,1)}, u32[]{:S(2)}) copy-start(bf16[1,4,192,768]{3,2,1,0:T(8,128)(2,1)} %param.6) | copy-start | bytes 3538948
  0.6 24.9 %slice-start = ((f32[2,768]{1,0:T(2,128)}), f32[1,768]{1,0:T(1,128)S(1)}, s32[]{:S(2)}) async-start(f32[2,768]{1,0:T(2,128)} %param.8), calls=%async_computation.4 | async-start | bytes 6144 | tf_op jit(solution)/shard_map/slice | solution.py:101
  1.9 23.7 %collective-permute-start.1 = (f32[1,192,768]{2,1,0:T(8,128)S(1)}, f32[1,192,768]{2,1,0:T(8,128)S(1)}, u32[]{:S(2)}, u32[]{:S(2)}) collective-permute-start(f32[1,192,768]{2,1,0:T(8,128)S(1)} %get-tuple-element.48), channel_id=1, source_target_pairs={{0,256},{256,0},{1,257},{257,1},{2,258},{258,2},{3,259},{259,3},{4... | collective-permute-start | bytes 1769480 | tf_op jit(solution)/shard_map/ppermute | solution.py:89
  13.4 32.3 %collective-permute-start = (f32[1,192,768]{2,1,0:T(8,128)S(1)}, f32[1,192,768]{2,1,0:T(8,128)S(1)}, u32[]{:S(2)}, u32[]{:S(2)}) collective-permute-start(f32[1,192,768]{2,1,0:T(8,128)S(1)} %get-tuple-element.49), channel_id=1, source_target_pairs={{0,256},{256,0},{1,257},{257,1},{2,258},{258,2},{3,259},{259,3},{4... | collective-permute-start | bytes 1769480 | tf_op jit(solution)/shard_map/ppermute | solution.py:89
  45.6 36.8 %copy-start.5 = (f32[2,192]{1,0:T(2,128)S(1)}, f32[2,192]{1,0:T(2,128)}, u32[]{:S(2)}) copy-start(f32[2,192]{1,0:T(2,128)} %param.9) | copy-start | bytes 4612
  45.7 49.8 %copy-start.4 = (f32[2,768]{1,0:T(2,128)S(1)}, f32[2,768]{1,0:T(2,128)}, u32[]{:S(2)}) copy-start(f32[2,768]{1,0:T(2,128)} %param.8) | copy-start | bytes 18436
  45.8 60.6 %copy-start = (f32[2,192,768]{2,1,0:T(8,128)S(1)}, f32[2,192,768]{2,1,0:T(8,128)}, u32[]{:S(2)}) copy-start(f32[2,192,768]{2,1,0:T(8,128)} %params_ref.1) | copy-start | bytes 3538948
  82.4 25.7 %copy-start.2 = (f32[2,192]{1,0:T(2,128)}, f32[2,192]{1,0:T(2,128)S(1)}, u32[]{:S(2)}) copy-start(f32[2,192]{1,0:T(2,128)S(1)} %fusion.3.cols_ref) | copy-start | bytes 4612
  95.7 12.4 %copy-start.1 = (f32[2,768]{1,0:T(2,128)}, f32[2,768]{1,0:T(2,128)S(1)}, u32[]{:S(2)}) copy-start(f32[2,768]{1,0:T(2,128)S(1)} %get-tuple-element.47.rows_ref) | copy-start | bytes 18436
